TPU v7x, 32 devices: a whole 2x2x4 slice. The times are simulated.
32 devices in a mesh: dm: 16 (over z, x, core), beam: 2 (over y).
Axes of the slice: x: 2, y: 2, z: 4, core: 2. Of those that a mesh axis runs over, the one named last changes fastest.
Arguments:
- voltages: bfloat16 [4096, 2, 2, 256], P(('beam', 'dm')), may hold values from -6 to 6
- responses: bfloat16 [64, 4096, 2, 256], P('dm', 'beam'), may hold values from -6 to 6
- chirp_len: int32 [64], P('dm'), may hold values from 1 to 128, as said below
Outputs:
- detected: bfloat16 [64, 2, 262144], P('dm', 'beam')
Inputs may be any that keep to these rules, and one draw needn't show every extreme that they name: `chirp_len`: some trial has the longest chirp 256 // 2 and some trial a chirp of 1 sample.
All inputs are finite; a program needn't handle non-finite values.
Results may differ from a plain program's by a relative error of at most 0.0054.
Values may be sent and summed in bfloat16 or wider, within the bound.
A program may use at most 128 MiB of HBM per device.

v0:
```python
import math

import jax
import jax.numpy as jnp
from jax import lax
from jax.sharding import PartitionSpec as P

RATE = 4


def dft_tables(length):
    sample = jnp.arange(length, dtype=jnp.int32)
    phases = sample[:, None] * sample[None, :] % length
    angles = phases.astype(jnp.float32) * (2.0 * math.pi / length)
    cosine = jnp.cos(angles) / math.sqrt(length)
    sine_part = jnp.sin(angles) / math.sqrt(length)
    forward = jnp.concatenate(
        [jnp.concatenate([cosine, -sine_part], 1), jnp.concatenate([sine_part, cosine], 1)], 0
    )
    backward = jnp.concatenate(
        [jnp.concatenate([cosine, sine_part], 1), jnp.concatenate([-sine_part, cosine], 1)], 0
    )
    return (forward.astype(jnp.bfloat16), backward.astype(jnp.bfloat16))


def spectrum(signal, forward):
    length = signal.shape[-1]
    flattened = signal.reshape(-1, 2 * length)
    result = jnp.dot(flattened, forward, preferred_element_type=jnp.float32)
    return result.astype(jnp.bfloat16).reshape(signal.shape)


def detect(spectra, response, lengths, backward, rate):
    chans = spectra.shape[0]
    beam_count = spectra.shape[1]
    length = spectra.shape[-1]
    samples_out = length // rate
    spec_re = spectra[:, :, 0, :].astype(jnp.float32)
    spec_im = spectra[:, :, 1, :].astype(jnp.float32)
    sample = jnp.arange(length, dtype=jnp.int32)

    def one_trial(trial):
        filter_row, chirp = trial
        resp_re = filter_row[:, 0, :].astype(jnp.float32)[:, None, :]
        resp_im = filter_row[:, 1, :].astype(jnp.float32)[:, None, :]
        real_part = resp_re * spec_re - resp_im * spec_im
        imag_part = resp_re * spec_im + resp_im * spec_re
        joined = jnp.concatenate([real_part, imag_part], -1).astype(jnp.bfloat16)
        series = jnp.dot(
            joined.reshape(-1, 2 * length), backward, preferred_element_type=jnp.float32
        )
        series = series.reshape(chans, beam_count, 2 * length)
        powers = series[..., :length] ** 2 + series[..., length:] ** 2
        valid_mask = sample >= chirp
        powers = jnp.where(valid_mask[None, None, :], powers, jnp.float32(0.0))
        binned = powers.reshape(chans, beam_count, samples_out, rate).sum(-1) / rate
        return jnp.transpose(binned, (1, 0, 2)).astype(jnp.bfloat16)

    return lax.map(one_trial, (response, lengths))


def shards(voltages, responses, chirp_len):
    length = voltages.shape[-1]
    forward, backward = dft_tables(length)
    trial_count = responses.shape[0]
    prepared = spectrum(lax.all_gather(voltages, "dm", axis=0, tiled=True), forward)
    detected = detect(prepared, responses, chirp_len, backward, RATE)
    flattened = detected.reshape(trial_count, detected.shape[1], -1)
    return lax.all_to_all(flattened, "beam", split_axis=1, concat_axis=2, tiled=True)


def solution(mesh):
    placed = (P(("beam", "dm"), None, None, None), P("dm", "beam", None, None), P("dm"))
    return jax.shard_map(
        shards, mesh=mesh, in_specs=placed, out_specs=P("dm", "beam", None), check_vma=False
    )
```

profile of v0, /device:TPU:0, one launch (start us, length us, event | category | flops | bytes accessed | tf_op | source)
XLA Modules:
  0.0 244.2 jit_solution(5988465926428411201)
XLA Ops:
  10.2 52.6 %all-gather.2.cloned.1.call-done = bf16[2048,2,2,256]{3,2,1,0:T(2,128)(2,1)} async-done(((bf16[128,2,2,256]{3,2,1,0:T(2,128)(2,1)}), bf16[2048,2,2,256]{3,2,1,0:T(2,128)(2,1)}) %all-gather.2.cloned.1.call-update) | async-done | bytes 4194320 | tf_op jit(solution)/shard_map/all_gather | solution.py:66
  62.8 2.9 %copy.22 = bf16[512,8,2,256]{3,1,2,0:T(8,128)(2,1)S(1)} copy(bf16[512,8,2,256]{3,2,1,0:T(2,128)(2,1)} %bitcast.56) | data formatting | bytes 8388608
  65.7 4.4 %fusion.14 = bf16[4096,512]{0,1:T(8,128)(2,1)} fusion(bf16[4096,512]{1,0:T(8,128)(2,1)S(1)} %bitcast.57, bf16[256,256]{0,1:T(8,128)(2,1)S(1)} %get-tuple-element.106, bf16[256,256]{0,1:T(8,128)(2,1)S(1)} %fusion.26, bf16[256,256]{0,1:T(8,128)(2,1)S(1)} %get-tuple-element.105), kind=kOutput, calls=%fused_computation.24 | convolution fusion | flops 2151677952 | bytes 8781824 | tf_op jit(solution)/shard_map/dot_general | solution.py:29
  70.1 6.5 %copy.11 = bf16[4096,512]{1,0:T(8,128)(2,1)} copy(bf16[4096,512]{0,1:T(8,128)(2,1)} %fusion.14) | data formatting | bytes 8388608 | tf_op jit(solution)/shard_map/convert_element_type | solution.py:30
  76.5 7.0 %reshape.32 = bf16[2048,2,2,256]{3,2,1,0:T(2,128)(2,1)} reshape(bf16[4096,512]{1,0:T(8,128)(2,1)} %copy.11) | data formatting | bytes 8388608 | tf_op jit(solution)/shard_map/reshape | solution.py:30
  83.5 8.8 %slice_convert_fusion = (f32[2048,2,1,256]{3,2,1,0:T(1,128)S(1)}, f32[2048,2,1,256]{3,2,1,0:T(1,128)S(1)}) fusion(bf16[2048,2,2,256]{3,2,1,0:T(2,128)(2,1)} %reshape.32), kind=kLoop, calls=%fused_computation.25 | loop fusion | flops 2097152 | bytes 12582912 | tf_op jit(solution)/shard_map/convert_element_type | solution.py:39
  92.3 2.3 copy.27
  94.7 2.3 copy.28
  96.9 103.5 %while.11 = (s32[]{:T(128)}, bf16[4,2,2048,64]{2,3,1,0:T(8,128)(2,1)S(1)}, s32[4]{0:T(128)S(1)}, bf16[4,2048,2,256]{3,2,1,0:T(2,128)(2,1)}, f32[2048,2,256]{2,0,...) while((s32[]{:T(128)}, ...), condition=%wide.region_2.3_spmd.clone, body=%wide.region_0.2_spmd.clone.sunk | while | flops 2170814720 | bytes 105906848 | solution.py:59
  96.9 3.2 %constant_dynamic-slice_fusion.2 = bf16[1,2048,2,256]{3,2,1,0:T(2,128)(2,1)S(1)} fusion(bf16[4,2048,2,256]{3,2,1,0:T(2,128)(2,1)} %get-tuple-element.179, s32[]{:T(128)} %get-tuple-element.167), kind=kLoop, calls=%fused_computation.21.clone.1 | loop fusion | bytes 4194308 | tf_op jit(solution)/shard_map/while/body/jit(dynamic_index_in_dim)/dynamic_slice | solution.py:59
  105.0 3.4 %fusion.38 = f32[2048,2,512]{0,2,1:T(8,128)S(1)} fusion(bf16[2048,2,256]{2,0,1:T(8,128)(2,1)S(1)} %get-tuple-element.156, bf16[2048,2,256]{2,0,1:T(8,128)(2,1)S(1)} %get-tuple-element.157, bf16[512,512]{0,1:T(8,128)(2,1)} %get-tuple-element.182), kind=kOutput, calls=%fused_computation.5.clone.1 | convolution fusion | flops 2155872256 | bytes 13107200 | tf_op jit(solution)/shard_map/while/body/eval_jaxpr/dot_general | solution.py:49
  109.7 3.0 %fusion.39 = f32[2048,2,256]{0,2,1:T(8,128)} fusion(f32[2048,2,512]{0,2,1:T(8,128)S(1)} %fusion.38, pred[256]{0:T(512)(128)(4,1)S(1)} %iota_compare_fusion.2), kind=kLoop, calls=%fused_computation.3.clone.1 | loop fusion | flops 4194304 | bytes 12583168 | tf_op jit(solution)/shard_map/while/body/eval_jaxpr/jit(_where)/select_n | solution.py:55
  112.6 5.2 %reshape.44 = f32[2048,2,64,4]{0,3,2,1:T(4,128)} reshape(f32[2048,2,256]{0,2,1:T(8,128)} %fusion.39) | data formatting | bytes 8388608 | tf_op jit(solution)/shard_map/while/body/eval_jaxpr/reshape | solution.py:56
  117.8 4.9 %reduce_sum.11 = f32[2048,2,64]{0,2,1:T(8,128)S(1)} reduce(f32[2048,2,64,4]{0,3,2,1:T(4,128)} %reshape.44, f32[]{:T(128)} %constant.29.clone.3..sunk), dimensions={3}, to_apply=%region_1.1 | reduce | flops 786432 | bytes 5242884 | tf_op jit(solution)/shard_map/while/body/eval_jaxpr/reduce_sum | solution.py:56
  122.8 3.2 %constant_dynamic-slice_fusion.2 = bf16[1,2048,2,256]{3,2,1,0:T(2,128)(2,1)S(1)} fusion(bf16[4,2048,2,256]{3,2,1,0:T(2,128)(2,1)} %get-tuple-element.179, s32[]{:T(128)} %get-tuple-element.167), kind=kLoop, calls=%fused_computation.21.clone.1 | loop fusion | bytes 4194308 | tf_op jit(solution)/shard_map/while/body/jit(dynamic_index_in_dim)/dynamic_slice | solution.py:59
  130.9 3.4 %fusion.38 = f32[2048,2,512]{0,2,1:T(8,128)S(1)} fusion(bf16[2048,2,256]{2,0,1:T(8,128)(2,1)S(1)} %get-tuple-element.156, bf16[2048,2,256]{2,0,1:T(8,128)(2,1)S(1)} %get-tuple-element.157, bf16[512,512]{0,1:T(8,128)(2,1)} %get-tuple-element.182), kind=kOutput, calls=%fused_computation.5.clone.1 | convolution fusion | flops 2155872256 | bytes 13107200 | tf_op jit(solution)/shard_map/while/body/eval_jaxpr/dot_general | solution.py:49
  135.6 3.0 %fusion.39 = f32[2048,2,256]{0,2,1:T(8,128)} fusion(f32[2048,2,512]{0,2,1:T(8,128)S(1)} %fusion.38, pred[256]{0:T(512)(128)(4,1)S(1)} %iota_compare_fusion.2), kind=kLoop, calls=%fused_computation.3.clone.1 | loop fusion | flops 4194304 | bytes 12583168 | tf_op jit(solution)/shard_map/while/body/eval_jaxpr/jit(_where)/select_n | solution.py:55
  138.5 5.2 %reshape.44 = f32[2048,2,64,4]{0,3,2,1:T(4,128)} reshape(f32[2048,2,256]{0,2,1:T(8,128)} %fusion.39) | data formatting | bytes 8388608 | tf_op jit(solution)/shard_map/while/body/eval_jaxpr/reshape | solution.py:56
  143.7 4.9 %reduce_sum.11 = f32[2048,2,64]{0,2,1:T(8,128)S(1)} reduce(f32[2048,2,64,4]{0,3,2,1:T(4,128)} %reshape.44, f32[]{:T(128)} %constant.29.clone.3..sunk), dimensions={3}, to_apply=%region_1.1 | reduce | flops 786432 | bytes 5242884 | tf_op jit(solution)/shard_map/while/body/eval_jaxpr/reduce_sum | solution.py:56
  148.7 3.2 %constant_dynamic-slice_fusion.2 = bf16[1,2048,2,256]{3,2,1,0:T(2,128)(2,1)S(1)} fusion(bf16[4,2048,2,256]{3,2,1,0:T(2,128)(2,1)} %get-tuple-element.179, s32[]{:T(128)} %get-tuple-element.167), kind=kLoop, calls=%fused_computation.21.clone.1 | loop fusion | bytes 4194308 | tf_op jit(solution)/shard_map/while/body/jit(dynamic_index_in_dim)/dynamic_slice | solution.py:59
  156.8 3.4 %fusion.38 = f32[2048,2,512]{0,2,1:T(8,128)S(1)} fusion(bf16[2048,2,256]{2,0,1:T(8,128)(2,1)S(1)} %get-tuple-element.156, bf16[2048,2,256]{2,0,1:T(8,128)(2,1)S(1)} %get-tuple-element.157, bf16[512,512]{0,1:T(8,128)(2,1)} %get-tuple-element.182), kind=kOutput, calls=%fused_computation.5.clone.1 | convolution fusion | flops 2155872256 | bytes 13107200 | tf_op jit(solution)/shard_map/while/body/eval_jaxpr/dot_general | solution.py:49
  161.4 3.0 %fusion.39 = f32[2048,2,256]{0,2,1:T(8,128)} fusion(f32[2048,2,512]{0,2,1:T(8,128)S(1)} %fusion.38, pred[256]{0:T(512)(128)(4,1)S(1)} %iota_compare_fusion.2), kind=kLoop, calls=%fused_computation.3.clone.1 | loop fusion | flops 4194304 | bytes 12583168 | tf_op jit(solution)/shard_map/while/body/eval_jaxpr/jit(_where)/select_n | solution.py:55
  164.4 5.2 %reshape.44 = f32[2048,2,64,4]{0,3,2,1:T(4,128)} reshape(f32[2048,2,256]{0,2,1:T(8,128)} %fusion.39) | data formatting | bytes 8388608 | tf_op jit(solution)/shard_map/while/body/eval_jaxpr/reshape | solution.py:56
  169.6 4.9 %reduce_sum.11 = f32[2048,2,64]{0,2,1:T(8,128)S(1)} reduce(f32[2048,2,64,4]{0,3,2,1:T(4,128)} %reshape.44, f32[]{:T(128)} %constant.29.clone.3..sunk), dimensions={3}, to_apply=%region_1.1 | reduce | flops 786432 | bytes 5242884 | tf_op jit(solution)/shard_map/while/body/eval_jaxpr/reduce_sum | solution.py:56
  174.6 3.2 %constant_dynamic-slice_fusion.2 = bf16[1,2048,2,256]{3,2,1,0:T(2,128)(2,1)S(1)} fusion(bf16[4,2048,2,256]{3,2,1,0:T(2,128)(2,1)} %get-tuple-element.179, s32[]{:T(128)} %get-tuple-element.167), kind=kLoop, calls=%fused_computation.21.clone.1 | loop fusion | bytes 4194308 | tf_op jit(solution)/shard_map/while/body/jit(dynamic_index_in_dim)/dynamic_slice | solution.py:59
  182.6 3.4 %fusion.38 = f32[2048,2,512]{0,2,1:T(8,128)S(1)} fusion(bf16[2048,2,256]{2,0,1:T(8,128)(2,1)S(1)} %get-tuple-element.156, bf16[2048,2,256]{2,0,1:T(8,128)(2,1)S(1)} %get-tuple-element.157, bf16[512,512]{0,1:T(8,128)(2,1)} %get-tuple-element.182), kind=kOutput, calls=%fused_computation.5.clone.1 | convolution fusion | flops 2155872256 | bytes 13107200 | tf_op jit(solution)/shard_map/while/body/eval_jaxpr/dot_general | solution.py:49
  187.3 3.0 %fusion.39 = f32[2048,2,256]{0,2,1:T(8,128)} fusion(f32[2048,2,512]{0,2,1:T(8,128)S(1)} %fusion.38, pred[256]{0:T(512)(128)(4,1)S(1)} %iota_compare_fusion.2), kind=kLoop, calls=%fused_computation.3.clone.1 | loop fusion | flops 4194304 | bytes 12583168 | tf_op jit(solution)/shard_map/while/body/eval_jaxpr/jit(_where)/select_n | solution.py:55
  190.3 5.2 %reshape.44 = f32[2048,2,64,4]{0,3,2,1:T(4,128)} reshape(f32[2048,2,256]{0,2,1:T(8,128)} %fusion.39) | data formatting | bytes 8388608 | tf_op jit(solution)/shard_map/while/body/eval_jaxpr/reshape | solution.py:56
  195.5 4.9 %reduce_sum.11 = f32[2048,2,64]{0,2,1:T(8,128)S(1)} reduce(f32[2048,2,64,4]{0,3,2,1:T(4,128)} %reshape.44, f32[]{:T(128)} %constant.29.clone.3..sunk), dimensions={3}, to_apply=%region_1.1 | reduce | flops 786432 | bytes 5242884 | tf_op jit(solution)/shard_map/while/body/eval_jaxpr/reduce_sum | solution.py:56
  200.4 3.2 %copy.19 = bf16[4,2,2048,64]{3,2,0,1:T(8,128)(2,1)} copy(bf16[4,2,2048,64]{2,3,1,0:T(8,128)(2,1)S(1)} %get-tuple-element.47) | data formatting | bytes 4194304 | tf_op jit(solution)/shard_map/reshape | solution.py:68
  203.6 4.3 %reshape.42 = bf16[4,2,131072]{2,0,1:T(4,128)(2,1)S(1)} reshape(bf16[4,2,2048,64]{3,2,0,1:T(8,128)(2,1)} %copy.19) | data formatting | bytes 4194304 | tf_op jit(solution)/shard_map/reshape | solution.py:68
  207.9 28.1 %all_to_all.12 = bf16[4,2,131072]{2,0,1:T(4,128)(2,1)S(1)} all-to-all(bf16[4,2,131072]{2,0,1:T(4,128)(2,1)S(1)} %reshape.42), channel_id=1, replica_groups=mesh['dm'=16,'beam'=2] {'beam'}, dimensions={1} | all-to-all | bytes 4194304 | tf_op jit(solution)/shard_map/all_to_all | solution.py:69
  (49 shorter events, 29.4 us)
Async XLA Ops:
  6.5 56.3 %all-gather.2.cloned.1.call-start = ((), (), s32[]{:S(2)}) async-start(), calls=%async_computation.1 | async-start | bytes 4456448 | tf_op jit(solution)/shard_map/all_gather | solution.py:66
  94.6 2.3 copy-start.2
  100.2 2.2 copy-start.1
  100.5 3.2 %copy-start = (f32[2048,2,256]{2,0,1:T(8,128)S(1)}, f32[2048,2,256]{2,0,1:T(8,128)}, u32[]{:S(2)}) copy-start(f32[2048,2,256]{2,0,1:T(8,128)} %get-tuple-element.181) | copy-start | bytes 12582916 | tf_op jit(solution)/shard_map/while
  126.1 2.2 copy-start.1
  126.3 3.2 %copy-start = (f32[2048,2,256]{2,0,1:T(8,128)S(1)}, f32[2048,2,256]{2,0,1:T(8,128)}, u32[]{:S(2)}) copy-start(f32[2048,2,256]{2,0,1:T(8,128)} %get-tuple-element.181) | copy-start | bytes 12582916 | tf_op jit(solution)/shard_map/while
  151.9 2.2 copy-start.1
  152.2 3.2 %copy-start = (f32[2048,2,256]{2,0,1:T(8,128)S(1)}, f32[2048,2,256]{2,0,1:T(8,128)}, u32[]{:S(2)}) copy-start(f32[2048,2,256]{2,0,1:T(8,128)} %get-tuple-element.181) | copy-start | bytes 12582916 | tf_op jit(solution)/shard_map/while
  177.8 2.2 copy-start.1
  178.1 3.2 %copy-start = (f32[2048,2,256]{2,0,1:T(8,128)S(1)}, f32[2048,2,256]{2,0,1:T(8,128)}, u32[]{:S(2)}) copy-start(f32[2048,2,256]{2,0,1:T(8,128)} %get-tuple-element.181) | copy-start | bytes 12582916 | tf_op jit(solution)/shard_map/while
Sparse Core Ops, SparseCore 0:
  9.5 53.2 all-gather.1
where the time goes:
time: 246 us; the launch traced here: 244 us
  local copies, waits for them, and re-layouts  78.6 us (32%)
  waiting for transfers between devices  53.3 us (22%)
  other arithmetic  52.3 us (21%)
  blocking collectives  28.1 us (11%)
  matrix products  18 us (7%)
  between operations  13.4 us (5%)
    all_gather x1, waiting for transfers between devices, shards(): lax.all_gather(voltages, 'dm', axis=0, tiled=True)  52.6 us
    all_to_all x1, blocking collectives, shards(): lax.all_to_all(flattened, 'beam', split_axis=1, concat_axis=2, tiled=True)  28.1 us
    reshape x4, local copies, waits for them, and re-layouts, one_trial(): binned = powers.reshape(chans, beam_count, samples_out, rate).sum(-1) / rate  20.7 us
    reduce_sum x4, other arithmetic, one_trial(): binned = powers.reshape(chans, beam_count, samples_out, rate).sum(-1) / rate  19.5 us
    dynamic_slice x12, local copies, waits for them, and re-layouts, detect(): return lax.map(one_trial, (response, lengths))  16.6 us
    dot_general x4, matrix products, one_trial(): jnp.dot(joined.reshape(-1, 2 * length), backward, preferred_element_type=...  13.7 us
    select_n x4, other arithmetic, one_trial(): powers = jnp.where(valid_mask[None, None, :], powers, jnp.float32(0.0))  11.9 us
    while x16, local copies, waits for them, and re-layouts  11.6 us
  transfers between devices with their start and end apart: 1, of which 1 were waited for; matrix products, arithmetic and copies ran while one was open for 1% of the time, Pallas kernels for 0%

commit v1 on v0

v1 whole, which is shorter than its diff:
```python
import functools
import math

import jax
import jax.numpy as jnp
import ml_dtypes
import numpy as np
from jax import lax
from jax.experimental import pallas as pl
from jax.experimental.pallas import tpu as pltpu
from jax.sharding import PartitionSpec as P

RATE = 4
LANES = 128
MESH = pl.DeviceIdType.MESH


def dft_tables(length):
    sample = np.arange(length)
    angles = (sample[:, None] * sample[None, :] % length) * (2.0 * math.pi / length)
    cosine = np.cos(angles) / math.sqrt(length)
    sine = np.sin(angles) / math.sqrt(length)
    forward = np.block([[cosine, -sine], [sine, cosine]])
    order = sample.reshape(-1, RATE).T.reshape(-1)
    cosine, sine = cosine[:, order], sine[:, order]
    backward = np.block([[cosine, sine], [-sine, cosine]])
    return [table.astype(np.float32).astype(ml_dtypes.bfloat16) for table in (forward, backward)]


def kernel(
    dm, beams, trials, chans, length,
    volt_ref, resp_ref, chirp_ref, fwd_ref, bwd_ref, out_ref,
    spec, resp, stage, rows_in, filt, rows_out,
    block_sem, far_sem, near_sem, core_sem, resp_sem, beam_send, beam_recv, own_sem,
):
    tiles = length // LANES
    half = chans // 2
    depth = dm // 4
    span = half * trials
    held = chans * tiles * 2
    me = lax.axis_index("dm")
    beam = lax.axis_index("beam")
    z, x, k = me // 4, (me // 2) % 2, me % 2

    def place(zz, xx, kk):
        return (zz * 2 + xx) * 2 + kk

    def plane(step):
        return (z + step) % depth

    def resp_copy(block):
        rows = pl.ds(block * held, held)
        return pltpu.make_async_copy(
            resp_ref.at[:, rows, :], resp.at[:, rows, :], resp_sem.at[block]
        )

    def send(block, sem, target):
        return pltpu.make_async_remote_copy(
            src_ref=spec.at[block],
            dst_ref=spec.at[block],
            send_sem=sem,
            recv_sem=block_sem.at[block],
            device_id={"dm": target},
            device_id_type=MESH,
        )

    def far(step):
        return send(me, far_sem.at[step - 1], place(plane(step), x, k))

    def near(step):
        return send(place(plane(step), x, k), near_sem.at[step], place(z, 1 - x, k))

    def across(step, side):
        column = (x + side) % 2
        block = place(plane(step), column, k)
        return send(block, core_sem.at[step * 2 + side], place(z, x, 1 - k))

    def arrived(block):
        pltpu.make_async_copy(spec.at[block], spec.at[block], block_sem.at[block]).wait()

    def beam_copy(offset, start, count):
        other = (beam + offset) % beams
        first = beam * (dm * span) + start
        return pltpu.make_async_remote_copy(
            src_ref=stage.at[other, pl.ds(start, count), :],
            dst_ref=out_ref.at[pl.ds(first, count), :],
            send_sem=beam_send.at[offset - 1],
            recv_sem=beam_recv.at[offset - 1],
            device_id={"beam": other},
            device_id_type=MESH,
        )

    def fetch(step, carry):
        plane_at = plane(step // 4)
        resp_copy(place(plane_at, (x + step % 4 // 2) % 2, (k + step % 2) % 2)).start()
        return carry

    lax.fori_loop(0, dm, fetch, 0)

    barrier = pltpu.get_barrier_semaphore()
    for step in range(1, depth):
        pl.semaphore_signal(
            barrier, inc=1, device_id={"dm": place(plane(step), x, k)}, device_id_type=MESH
        )
    pl.semaphore_signal(barrier, inc=1, device_id={"dm": place(z, 1 - x, k)}, device_id_type=MESH)
    pl.semaphore_signal(barrier, inc=1, device_id={"dm": place(z, x, 1 - k)}, device_id_type=MESH)
    for offset in range(1, beams):
        pl.semaphore_signal(
            barrier, inc=1, device_id={"beam": (beam + offset) % beams}, device_id_type=MESH
        )

    rows_in[...] = volt_ref[...].astype(jnp.float32)
    stride = 2 * beams * tiles * 2
    pieces = []
    for b in range(beams):
        for parity in range(2):
            first = (parity * beams + b) * tiles * 2
            pieces.append(jnp.concatenate(
                [rows_in[pl.ds(first + t * 2 + part, half, stride=stride), :]
                 for part in range(2) for t in range(tiles)], 1))
    signal = jnp.concatenate(pieces, 0).astype(jnp.bfloat16)
    spec[me] = jnp.dot(
        signal, fwd_ref[...], preferred_element_type=jnp.float32
    ).astype(jnp.bfloat16)

    pl.semaphore_wait(barrier, depth + beams)

    near(0).start()
    for step in range(1, depth):
        far(step).start()
    across(0, 0).start()

    column = lax.broadcasted_iota(jnp.int32, (1, length), 1)
    bins = length // RATE
    sample = column % bins * RATE + column // bins
    low = lax.broadcasted_iota(jnp.int32, (half, LANES), 1) < bins

    def detect(block):
        for d in range(trials):
            filt[d] = resp[d, pl.ds(block * held, held), :].astype(jnp.float32)
        for d in range(trials):
            taps = [[jnp.concatenate(
                [filt[d, pl.ds((parity * tiles + t) * 2 + part, half, stride=4 * tiles), :]
                 for t in range(tiles)], 1) for part in range(2)] for parity in range(2)]
            values = spec[block].astype(jnp.float32)
            pieces = []
            for b in range(beams):
                for parity in range(2):
                    at = (b * 2 + parity) * half
                    xr = values[at:at + half, :length]
                    xi = values[at:at + half, length:]
                    hr, hi = taps[parity]
                    pieces.append(
                        jnp.concatenate([hr * xr - hi * xi, hr * xi + hi * xr], 1)
                    )
            joined = jnp.concatenate(pieces, 0).astype(jnp.bfloat16)
            series = jnp.dot(joined, bwd_ref[...], preferred_element_type=jnp.float32)
            power = series[:, :length] * series[:, :length] + series[:, length:] * series[:, length:]
            power = jnp.where(sample >= chirp_ref[d], power, 0.0)
            total = power[:, :LANES]
            for t in range(1, tiles):
                total = total + power[:, t * LANES:(t + 1) * LANES]
            for b in range(beams):
                at = b * 2 * half
                even = total[at:at + half]
                odd = total[at + half:at + 2 * half]
                straight = jnp.where(low, even, odd)
                turned = pltpu.roll(jnp.where(low, odd, even), bins, 1)
                rows_out[b, pl.ds(d, half, stride=trials), :] = (straight + turned) * (1.0 / RATE)
        for b in range(beams):
            stage[b, pl.ds(block * span, span), :] = rows_out[b].astype(jnp.bfloat16)

    def body(step, carry):
        group, turn = step // 4, step % 4
        block = place(plane(group), (x + turn // 2) % 2, (k + turn % 2) % 2)

        @pl.when(turn > 0)
        def _():
            arrived(block)

        @pl.when(turn == 2)
        def _():
            across(group, 1).start()

        @pl.when((turn == 1) & (group < depth - 1))
        def _():
            arrived(place(plane(group + 1), x, k))
            near(group + 1).start()
            across(group + 1, 0).start()

        resp_copy(block).wait()
        detect(block)
        for offset in range(1, beams):
            beam_copy(offset, block * span, span).start()
        return carry

    lax.fori_loop(0, dm, body, 0)

    own = pltpu.make_async_copy(
        stage.at[beam], out_ref.at[pl.ds(beam * (dm * span), dm * span), :], own_sem
    )
    own.start()

    for step in range(1, depth):
        far(step).wait_send()
    for step in range(depth):
        near(step).wait_send()
        across(step, 0).wait_send()
        across(step, 1).wait_send()
    own.wait()
    for offset in range(1, beams):
        whole = beam_copy(offset, 0, dm * span)
        whole.wait_send()
        whole.wait_recv()


def shards(dm, beams, voltages, responses, chirp_len):
    chans, _, _, length = voltages.shape
    trials, group = responses.shape[:2]
    tiles = length // LANES
    forward, backward = dft_tables(length)

    def tiled(array):
        head = array.shape[:-2]
        array = array.reshape(head + (2, tiles, LANES))
        return jnp.swapaxes(array, -2, -3)

    volt = tiled(voltages).reshape(chans * beams * tiles * 2, LANES)
    resp = tiled(responses).reshape(trials, group * tiles * 2, LANES)
    span = chans // 2 * trials
    rows = beams * dm * span
    vmem = pl.BlockSpec(memory_space=pltpu.VMEM)
    anywhere = pl.BlockSpec(memory_space=pl.ANY)
    flops = 2 * (trials * group + chans) * beams * (2 * length) ** 2
    out = pl.pallas_call(
        functools.partial(kernel, dm, beams, trials, chans, length),
        out_shape=jax.ShapeDtypeStruct((rows, LANES), jnp.bfloat16),
        in_specs=[vmem, anywhere, pl.BlockSpec(memory_space=pltpu.SMEM), vmem, vmem],
        out_specs=anywhere,
        scratch_shapes=[
            pltpu.VMEM((dm, beams * chans, 2 * length), jnp.bfloat16),
            pltpu.VMEM(resp.shape, jnp.bfloat16),
            pltpu.VMEM((beams, dm * span, LANES), jnp.bfloat16),
            pltpu.VMEM(volt.shape, jnp.float32),
            pltpu.VMEM((trials, chans * tiles * 2, LANES), jnp.float32),
            pltpu.VMEM((beams, span, LANES), jnp.float32),
            pltpu.SemaphoreType.DMA((dm,)),
            pltpu.SemaphoreType.DMA((dm // 4,)),
            pltpu.SemaphoreType.DMA((dm // 4,)),
            pltpu.SemaphoreType.DMA((dm // 2,)),
            pltpu.SemaphoreType.DMA((dm,)),
            pltpu.SemaphoreType.DMA((beams,)),
            pltpu.SemaphoreType.DMA((beams,)),
            pltpu.SemaphoreType.DMA,
        ],
        compiler_params=pltpu.CompilerParams(
            collective_id=0, has_side_effects=True, vmem_limit_bytes=48 * 2**20
        ),
        cost_estimate=pl.CostEstimate(
            flops=flops, bytes_accessed=resp.size * 2 + rows * LANES * 2, transcendentals=0
        ),
    )(volt, resp, chirp_len, jnp.asarray(forward), jnp.asarray(backward))
    out = out.reshape(-1, trials, LANES)
    return jnp.swapaxes(out, 0, 1).reshape(trials, 1, -1)


def solution(mesh):
    placed = (P(("beam", "dm"), None, None, None), P("dm", "beam", None, None), P("dm"))
    return jax.shard_map(
        functools.partial(shards, mesh.shape["dm"], mesh.shape["beam"]),
        mesh=mesh, in_specs=placed, out_specs=P("dm", "beam", None), check_vma=False,
    )
```

time: 246 us -> 58.3 us (0.24)
  the two profiles are of different devices: /device:TPU:0 before, /device:TPU:9 now
where the time goes in v1:
time: 58.3 us; the launch traced here: 58 us
  Pallas kernels  53 us (91%)
  local copies, waits for them, and re-layouts  5.01 us (9%)
    pallas_call x1, Pallas kernels, shards(): pl.pallas_call(functools.partial(kernel, dm, beams, trials, chans, length...  53 us
    unnamed x9, local copies, waits for them, and re-layouts  5.01 us

profile of v1, /device:TPU:9, one launch (start us, length us, event | category | flops | bytes accessed | tf_op | source)
XLA Modules:
  0.0 58.0 jit_solution(464271269256347327)
XLA Ops:
  0.0 0.0 copy-start
  0.0 0.9 %copy-done = bf16[128,2,2,256]{3,2,1,0:T(2,128)(2,1)S(1)} copy-done((bf16[128,2,2,256]{3,2,1,0:T(2,128)(2,1)S(1)}, bf16[128,2,2,256]{3,2,1,0:T(2,128)(2,1)}, u32[]{:S(2)}) %copy-start) | copy-done | bytes 262168
  1.0 0.0 copy-start.1
  1.0 0.7 %copy-done.1 = s32[4]{0:T(128)S(1)} copy-done((s32[4]{0:T(128)S(1)}, s32[4]{0:T(128)}, u32[]{:S(2)}) %copy-start.1) | copy-done | bytes 40
  1.6 0.0 copy-start.2
  1.6 1.0 %copy-done.2 = bf16[512,512]{1,0:T(8,128)(2,1)S(1)} copy-done((bf16[512,512]{1,0:T(8,128)(2,1)S(1)}, bf16[512,512]{1,0:T(8,128)(2,1)}, u32[]{:S(2)}) %copy-start.2) | copy-done | bytes 524312
  2.6 0.0 copy-start.3
  2.7 1.0 %copy-done.3 = bf16[512,512]{1,0:T(8,128)(2,1)S(1)} copy-done((bf16[512,512]{1,0:T(8,128)(2,1)S(1)}, bf16[512,512]{1,0:T(8,128)(2,1)}, u32[]{:S(2)}) %copy-start.3) | copy-done | bytes 524312
  3.7 53.0 %shard_map.55 = bf16[8192,128]{1,0:T(8,128)(2,1)S(1)} custom-call(bf16[1024,128]{1,0:T(8,128)(2,1)S(1)} %bitcast.16, bf16[4,8192,128]{2,1,0:T(8,128)(2,1)} %bitcast.17, s32[4]{0:T(128)S(1)} %copy-done.1, bf16[512,512]{1,0:T(8,128)(2,1)S(1)} %copy-done.3, bf16[512,512]{1,0:T(8,128)(2,1)S(1)} %copy-done.2), custom_call_target="tpu_custom_call" | custom-call | flops 8724152320 | bytes 10485760 | tf_op jit(solution)/shard_map/pallas_call | solution.py:235
  56.7 1.3 %copy.10 = bf16[4,1,262144]{2,0,1:T(4,128)(2,1)} copy(bf16[4,1,262144]{2,0,1:T(4,128)(2,1)S(1)} %bitcast.15) | data formatting | bytes 4194304
Async XLA Ops:
  0.0 0.9 %copy-start = (bf16[128,2,2,256]{3,2,1,0:T(2,128)(2,1)S(1)}, bf16[128,2,2,256]{3,2,1,0:T(2,128)(2,1)}, u32[]{:S(2)}) copy-start(bf16[128,2,2,256]{3,2,1,0:T(2,128)(2,1)} %param.5) | copy-start | bytes 786436
  1.0 0.7 %copy-start.1 = (s32[4]{0:T(128)S(1)}, s32[4]{0:T(128)}, u32[]{:S(2)}) copy-start(s32[4]{0:T(128)} %chirp_ref.1) | copy-start | bytes 52
  1.6 1.0 %copy-start.2 = (bf16[512,512]{1,0:T(8,128)(2,1)S(1)}, bf16[512,512]{1,0:T(8,128)(2,1)}, u32[]{:S(2)}) copy-start(bf16[512,512]{1,0:T(8,128)(2,1)} %constant.5.clone.bwd_ref) | copy-start | bytes 1572868
  2.6 1.0 %copy-start.3 = (bf16[512,512]{1,0:T(8,128)(2,1)S(1)}, bf16[512,512]{1,0:T(8,128)(2,1)}, u32[]{:S(2)}) copy-start(bf16[512,512]{1,0:T(8,128)(2,1)} %constant.4.clone.fwd_ref) | copy-start | bytes 1572868

commit v2 on v1

--- a/solution.py
+++ b/solution.py
@@ -29,9 +29,9 @@
 
 def kernel(
     dm, beams, trials, chans, length,
-    volt_ref, resp_ref, chirp_ref, fwd_ref, bwd_ref, out_ref,
-    spec, resp, stage, rows_in, filt, rows_out,
-    block_sem, far_sem, near_sem, core_sem, resp_sem, beam_send, beam_recv, own_sem,
+    volt_hbm, resp_ref, chirp_hbm, fwd_hbm, bwd_hbm, out_ref,
+    volt_ref, chirp_ref, fwd_ref, bwd_ref, spec, resp, stage, rows_in, filt, rows_out,
+    block_sem, up_sem, down_sem, near_sem, core_sem, resp_sem, beam_send, beam_recv, own_sem, in_sem,
 ):
     tiles = length // LANES
     half = chans // 2
@@ -45,8 +45,13 @@
     def place(zz, xx, kk):
         return (zz * 2 + xx) * 2 + kk
 
+    last = depth - 1
+    inner = jnp.minimum(z, last - z)
+    side = 1 - 2 * (2 * z // depth)
+
     def plane(step):
-        return (z + step) % depth
+        turns = z + (1 - 2 * (step % 2)) * ((step + 1) // 2)
+        return jnp.where(step <= 2 * inner, turns, z + side * (step - inner))
 
     def resp_copy(block):
         rows = pl.ds(block * held, held)
@@ -64,8 +69,11 @@
             device_id_type=MESH,
         )
 
-    def far(step):
-        return send(me, far_sem.at[step - 1], place(plane(step), x, k))
+    def up(origin):
+        return send(place(origin, x, k), up_sem.at[origin], place(z + 1, x, k))
+
+    def down(origin):
+        return send(place(origin, x, k), down_sem.at[origin], place(z - 1, x, k))
 
     def near(step):
         return send(place(plane(step), x, k), near_sem.at[step], place(z, 1 - x, k))
@@ -95,13 +103,30 @@
         resp_copy(place(plane_at, (x + step % 4 // 2) % 2, (k + step % 2) % 2)).start()
         return carry
 
+    inputs = [
+        pltpu.make_async_copy(source, target, in_sem.at[i])
+        for i, (source, target) in enumerate(
+            [(volt_hbm, volt_ref), (fwd_hbm, fwd_ref), (bwd_hbm, bwd_ref), (chirp_hbm, chirp_ref)]
+        )
+    ]
+    for copy in inputs:
+        copy.start()
     lax.fori_loop(0, dm, fetch, 0)
 
     barrier = pltpu.get_barrier_semaphore()
-    for step in range(1, depth):
+
+    @pl.when(z < last)
+    def _():
         pl.semaphore_signal(
-            barrier, inc=1, device_id={"dm": place(plane(step), x, k)}, device_id_type=MESH
-        )
+            barrier, inc=1, device_id={"dm": place(z + 1, x, k)}, device_id_type=MESH
+        )
+
+    @pl.when(z > 0)
+    def _():
+        pl.semaphore_signal(
+            barrier, inc=1, device_id={"dm": place(z - 1, x, k)}, device_id_type=MESH
+        )
+
     pl.semaphore_signal(barrier, inc=1, device_id={"dm": place(z, 1 - x, k)}, device_id_type=MESH)
     pl.semaphore_signal(barrier, inc=1, device_id={"dm": place(z, x, 1 - k)}, device_id_type=MESH)
     for offset in range(1, beams):
@@ -109,6 +134,8 @@
             barrier, inc=1, device_id={"beam": (beam + offset) % beams}, device_id_type=MESH
         )
 
+    inputs[0].wait()
+    inputs[1].wait()
     rows_in[...] = volt_ref[...].astype(jnp.float32)
     stride = 2 * beams * tiles * 2
     pieces = []
@@ -123,12 +150,20 @@
         signal, fwd_ref[...], preferred_element_type=jnp.float32
     ).astype(jnp.bfloat16)
 
-    pl.semaphore_wait(barrier, depth + beams)
+    pl.semaphore_wait(barrier, 1 + beams + jnp.minimum(z, 1) + jnp.minimum(last - z, 1))
+
+    @pl.when(z < last)
+    def _():
+        up(z).start()
+
+    @pl.when(z > 0)
+    def _():
+        down(z).start()
 
     near(0).start()
-    for step in range(1, depth):
-        far(step).start()
     across(0, 0).start()
+    inputs[2].wait()
+    inputs[3].wait()
 
     column = lax.broadcasted_iota(jnp.int32, (1, length), 1)
     bins = length // RATE
@@ -174,19 +209,34 @@
         group, turn = step // 4, step % 4
         block = place(plane(group), (x + turn // 2) % 2, (k + turn % 2) % 2)
 
-        @pl.when(turn > 0)
-        def _():
-            arrived(block)
-
-        @pl.when(turn == 2)
-        def _():
-            across(group, 1).start()
-
-        @pl.when((turn == 1) & (group < depth - 1))
-        def _():
-            arrived(place(plane(group + 1), x, k))
+        @pl.when((turn == 2) & (group < last) & (z > group))
+        def _():
+            arrived(place(z - group - 1, x, k))
+
+        @pl.when((turn == 2) & (group < last) & (z > group) & (z < last))
+        def _():
+            up(z - group - 1).start()
+
+        @pl.when((turn == 2) & (group < last) & (z + group < last))
+        def _():
+            arrived(place(z + group + 1, x, k))
+
+        @pl.when((turn == 2) & (group < last) & (z + group < last) & (z > 0))
+        def _():
+            down(z + group + 1).start()
+
+        @pl.when((turn == 2) & (group < last))
+        def _():
             near(group + 1).start()
             across(group + 1, 0).start()
+
+        @pl.when(turn > 0)
+        def _():
+            arrived(block)
+
+        @pl.when(turn == 2)
+        def _():
+            across(group, 1).start()
 
         resp_copy(block).wait()
         detect(block)
@@ -201,8 +251,15 @@
     )
     own.start()
 
-    for step in range(1, depth):
-        far(step).wait_send()
+    for step in range(depth):
+        @pl.when((z < last) & (z >= step))
+        def _(step=step):
+            up(step).wait_send()
+
+        @pl.when((z > 0) & (z <= step))
+        def _(step=step):
+            down(step).wait_send()
+
     for step in range(depth):
         near(step).wait_send()
         across(step, 0).wait_send()
@@ -229,15 +286,18 @@
     resp = tiled(responses).reshape(trials, group * tiles * 2, LANES)
     span = chans // 2 * trials
     rows = beams * dm * span
-    vmem = pl.BlockSpec(memory_space=pltpu.VMEM)
     anywhere = pl.BlockSpec(memory_space=pl.ANY)
     flops = 2 * (trials * group + chans) * beams * (2 * length) ** 2
     out = pl.pallas_call(
         functools.partial(kernel, dm, beams, trials, chans, length),
         out_shape=jax.ShapeDtypeStruct((rows, LANES), jnp.bfloat16),
-        in_specs=[vmem, anywhere, pl.BlockSpec(memory_space=pltpu.SMEM), vmem, vmem],
+        in_specs=[pl.BlockSpec(memory_space=pltpu.HBM)] * 5,
         out_specs=anywhere,
         scratch_shapes=[
+            pltpu.VMEM(volt.shape, jnp.bfloat16),
+            pltpu.SMEM(chirp_len.shape, jnp.int32),
+            pltpu.VMEM(forward.shape, jnp.bfloat16),
+            pltpu.VMEM(backward.shape, jnp.bfloat16),
             pltpu.VMEM((dm, beams * chans, 2 * length), jnp.bfloat16),
             pltpu.VMEM(resp.shape, jnp.bfloat16),
             pltpu.VMEM((beams, dm * span, LANES), jnp.bfloat16),
@@ -247,11 +307,13 @@
             pltpu.SemaphoreType.DMA((dm,)),
             pltpu.SemaphoreType.DMA((dm // 4,)),
             pltpu.SemaphoreType.DMA((dm // 4,)),
+            pltpu.SemaphoreType.DMA((dm // 4,)),
             pltpu.SemaphoreType.DMA((dm // 2,)),
             pltpu.SemaphoreType.DMA((dm,)),
             pltpu.SemaphoreType.DMA((beams,)),
             pltpu.SemaphoreType.DMA((beams,)),
             pltpu.SemaphoreType.DMA,
+            pltpu.SemaphoreType.DMA((4,)),
         ],
         compiler_params=pltpu.CompilerParams(
             collective_id=0, has_side_effects=True, vmem_limit_bytes=48 * 2**20

time: 58.3 us -> 43.5 us (0.75)
  the two profiles are of different devices: /device:TPU:9 before, /device:TPU:0 now
where the time goes in v2:
time: 43.5 us; the launch traced here: 43.3 us
  Pallas kernels  38.3 us (88%)
  local copies, waits for them, and re-layouts  5.01 us (12%)
    pallas_call x1, Pallas kernels, shards(): pl.pallas_call(functools.partial(kernel, dm, beams, trials, chans, length...  38.3 us
    unnamed x9, local copies, waits for them, and re-layouts  5.01 us

profile of v2, /device:TPU:0, one launch (start us, length us, event | category | flops | bytes accessed | tf_op | source)
XLA Modules:
  0.0 43.3 jit_solution(2402763431437734755)
XLA Ops:
  0.0 0.0 copy-start
  0.0 0.9 %copy-done = bf16[128,2,2,256]{3,2,1,0:T(2,128)(2,1)S(1)} copy-done((bf16[128,2,2,256]{3,2,1,0:T(2,128)(2,1)S(1)}, bf16[128,2,2,256]{3,2,1,0:T(2,128)(2,1)}, u32[]{:S(2)}) %copy-start) | copy-done | bytes 262168
  1.0 0.0 copy-start.1
  1.0 0.7 %copy-done.1 = s32[4]{0:T(128)S(1)} copy-done((s32[4]{0:T(128)S(1)}, s32[4]{0:T(128)}, u32[]{:S(2)}) %copy-start.1) | copy-done | bytes 40
  1.6 0.0 copy-start.2
  1.6 1.0 %copy-done.2 = bf16[512,512]{1,0:T(8,128)(2,1)S(1)} copy-done((bf16[512,512]{1,0:T(8,128)(2,1)S(1)}, bf16[512,512]{1,0:T(8,128)(2,1)}, u32[]{:S(2)}) %copy-start.2) | copy-done | bytes 524312
  2.6 0.0 copy-start.3
  2.7 1.0 %copy-done.3 = bf16[512,512]{1,0:T(8,128)(2,1)S(1)} copy-done((bf16[512,512]{1,0:T(8,128)(2,1)S(1)}, bf16[512,512]{1,0:T(8,128)(2,1)}, u32[]{:S(2)}) %copy-start.3) | copy-done | bytes 524312
  3.7 38.3 %shard_map.55 = bf16[8192,128]{1,0:T(8,128)(2,1)S(1)} custom-call(bf16[1024,128]{1,0:T(8,128)(2,1)S(1)} %bitcast.16, bf16[4,8192,128]{2,1,0:T(8,128)(2,1)} %bitcast.17, s32[4]{0:T(128)S(1)} %copy-done.1, bf16[512,512]{1,0:T(8,128)(2,1)S(1)} %copy-done.3, bf16[512,512]{1,0:T(8,128)(2,1)S(1)} %copy-done.2), custom_call_target="tpu_custom_call" | custom-call | flops 8724152320 | bytes 10485760 | tf_op jit(solution)/shard_map/pallas_call | solution.py:291
  42.0 1.3 %copy.10 = bf16[4,1,262144]{2,0,1:T(4,128)(2,1)} copy(bf16[4,1,262144]{2,0,1:T(4,128)(2,1)S(1)} %bitcast.15) | data formatting | bytes 4194304
Async XLA Ops:
  0.0 0.9 %copy-start = (bf16[128,2,2,256]{3,2,1,0:T(2,128)(2,1)S(1)}, bf16[128,2,2,256]{3,2,1,0:T(2,128)(2,1)}, u32[]{:S(2)}) copy-start(bf16[128,2,2,256]{3,2,1,0:T(2,128)(2,1)} %param.5) | copy-start | bytes 786436
  1.0 0.7 %copy-start.1 = (s32[4]{0:T(128)S(1)}, s32[4]{0:T(128)}, u32[]{:S(2)}) copy-start(s32[4]{0:T(128)} %chirp_hbm.1) | copy-start | bytes 52
  1.6 1.0 %copy-start.2 = (bf16[512,512]{1,0:T(8,128)(2,1)S(1)}, bf16[512,512]{1,0:T(8,128)(2,1)}, u32[]{:S(2)}) copy-start(bf16[512,512]{1,0:T(8,128)(2,1)} %constant.5.clone.bwd_hbm) | copy-start | bytes 1572868
  2.6 1.0 %copy-start.3 = (bf16[512,512]{1,0:T(8,128)(2,1)S(1)}, bf16[512,512]{1,0:T(8,128)(2,1)}, u32[]{:S(2)}) copy-start(bf16[512,512]{1,0:T(8,128)(2,1)} %constant.4.clone.fwd_hbm) | copy-start | bytes 1572868

commit v3 on v2

--- a/solution.py
+++ b/solution.py
@@ -316,7 +316,7 @@
             pltpu.SemaphoreType.DMA((4,)),
         ],
         compiler_params=pltpu.CompilerParams(
-            collective_id=0, has_side_effects=True, vmem_limit_bytes=48 * 2**20
+            collective_id=0, has_side_effects=True, vmem_limit_bytes=60 * 2**20
         ),
         cost_estimate=pl.CostEstimate(
             flops=flops, bytes_accessed=resp.size * 2 + rows * LANES * 2, transcendentals=0

time: 43.5 us -> 41.2 us (0.947)
  local copies, waits for them, and re-layouts: 5.01 us -> 2.94 us
    unnamed x9 -> x1, local copies, waits for them, and re-layouts: 5.01 us -> 2.94 us
where the time goes in v3:
time: 41.2 us; the launch traced here: 41 us
  Pallas kernels  38.1 us (92%)
  local copies, waits for them, and re-layouts  2.94 us (7%)
    pallas_call x1, Pallas kernels, shards(): pl.pallas_call(functools.partial(kernel, dm, beams, trials, chans, length...  38.1 us
    unnamed x1, local copies, waits for them, and re-layouts  2.94 us

profile of v3, /device:TPU:0, one launch (start us, length us, event | category | flops | bytes accessed | tf_op | source)
XLA Modules:
  0.0 41.0 jit_solution(11147743197412748512)
XLA Ops:
  0.0 38.1 %shard_map.55 = bf16[8192,128]{1,0:T(8,128)(2,1)} custom-call(bf16[1024,128]{1,0:T(8,128)(2,1)} %bitcast.17, bf16[4,8192,128]{2,1,0:T(8,128)(2,1)} %bitcast.16, s32[4]{0:T(128)} %chirp_hbm.1, bf16[512,512]{1,0:T(8,128)(2,1)} %constant.4.clone.fwd_hbm, bf16[512,512]{1,0:T(8,128)(2,1)} %constant.5.clone.bwd_hbm), custom_call_target="tpu_custom_call" | custom-call | flops 8724152320 | bytes 10485760 | tf_op jit(solution)/shard_map/pallas_call | solution.py:291
  38.1 2.9 %copy.10 = bf16[4,1,262144]{2,0,1:T(4,128)(2,1)} copy(bf16[4,1,262144]{2,0,1:T(4,128)(2,1)} %bitcast.15) | data formatting | bytes 4194304
